TPU v7x, 128 devices: a whole 4x4x4 slice. The times are simulated.
128 devices in a mesh: zero: 32 (over x, z, core), expert: 4 (over y).
Axes of the slice: x: 4, y: 4, z: 4, core: 2. Of those that a mesh axis runs over, the one named last changes fastest.
Arguments:
- grad: bfloat16 [48, 576, 7168], P('expert', 'zero'), may hold values from -6 to 6
- momentum: float32 [48, 576, 7168], P('expert', 'zero'), may hold values from -6 to 6
- backup: float32 [48, 576, 7168], P('expert', 'zero'), may hold values from -6 to 6
- recovery: int32 [4], replicated, may hold values from 0 to 31
Outputs:
- new_momentum: float32 [48, 576, 7168], P('expert', 'zero')
- update: bfloat16 [48, 576, 7168], P('expert', 'zero')
All inputs are finite; a program needn't handle non-finite values.
Results may differ from a plain program's by a relative error of at most 0.006.
Values may be sent and summed in bfloat16 or wider, within the bound.
A program may use at most 192 MiB of HBM per device.

v0:
```python
import jax
import jax.numpy as jnp
from jax import lax
from jax.sharding import PartitionSpec as P

MODEL_WIDTH = 7168
LATENT_KEY_WIDTH = 512
ROTARY_KEY_HEAD = 64
ITERS = 3


beta = 0.95
coef_a = 3.4445
coef_b = -4.775
coef_c = 2.0315
eps = 1e-07
highest = lax.Precision.HIGHEST


def shifted(value, axis, steps):
    count = lax.axis_size(axis)
    pairs = [(source, (source + steps) % count) for source in range(count)]
    return lax.ppermute(value, axis, pairs)


def mult(left, right):
    return jnp.einsum(
        "...ij,...jk->...ik", left, right, precision=highest, preferred_element_type=jnp.float32
    )


def gram_of(current):
    return jnp.einsum(
        "...ij,...kj->...ik",
        current,
        current,
        precision=highest,
        preferred_element_type=jnp.float32,
    )


def poly_chain(gram):
    order = gram.shape[-1]
    identity = jnp.eye(order, dtype=jnp.float32)
    product = jnp.broadcast_to(identity, gram.shape)
    for step in range(ITERS):
        poly = coef_a * identity + coef_b * gram + coef_c * mult(gram, gram)
        gram = mult(poly, mult(gram, poly))
        product = mult(poly, product)
    return product


def local(grad, momentum, backup, recovery):
    peers = lax.axis_size("zero")
    my_group = lax.axis_index("expert")
    copied = shifted(backup.astype(jnp.bfloat16), "expert", 1).astype(backup.dtype)
    shard_missing = lax.axis_index("zero") == recovery[my_group]
    live = jnp.where(shard_missing, copied, momentum)
    gradient_wide = grad.astype(jnp.float32)
    new_momentum = beta * live + gradient_wide
    blend = gradient_wide + beta * new_momentum
    count, rows, width = blend.shape
    scale_factor = 0.2 * max(LATENT_KEY_WIDTH + ROTARY_KEY_HEAD, MODEL_WIDTH) ** 0.5
    filler = jnp.zeros((peers - count, rows, width), jnp.float32)
    parcel = jnp.concatenate([blend, filler], axis=0)[:, None]
    held = lax.all_to_all(parcel, "zero", split_axis=0, concat_axis=2, tiled=True)
    norm = jnp.sqrt(jnp.sum(held * held, axis=(-2, -1), keepdims=True))
    start = held / (norm + eps)
    product = poly_chain(gram_of(start))
    result = (mult(product, start) * scale_factor).astype(jnp.bfloat16)
    returned = lax.all_to_all(result, "zero", split_axis=2, concat_axis=0, tiled=True)
    update = returned.reshape(peers, rows, width)[:count]
    return (new_momentum, update)


def solution(mesh):
    in_specs = (
        P("expert", "zero", None),
        P("expert", "zero", None),
        P("expert", "zero", None),
        P(),
    )
    out_specs = (P("expert", "zero", None), P("expert", "zero", None))
    return jax.shard_map(local, mesh=mesh, in_specs=in_specs, out_specs=out_specs, check_vma=False)
```

profile of v0, /device:TPU:33, one launch (start us, length us, event | category | flops | bytes accessed | tf_op | source)
XLA Modules:
  0.0 890.9 jit_solution(14982026954171370046)
XLA Ops:
  0.6 0.0 copy-start.1
  0.6 8.7 copy.23
  9.3 1.3 collective-permute-start
  10.6 0.0 copy-done.1
  10.6 0.6 dynamic_slice.3
  11.8 89.2 %collective-permute-done = bf16[12,18,7168]{2,0,1:T(8,128)(2,1)} collective-permute-done((bf16[12,18,7168]{2,0,1:T(8,128)(2,1)}, bf16[12,18,7168]{2,0,1:T(8,128)(2,1)}, u32[]{:S(2)}, u32[]{:S(2)}) %collective-permute-start) | collective-permute-done | bytes 3096608 | tf_op jit(solution)/shard_map/ppermute | solution.py:23
  101.0 14.5 %convert_add_fusion = (f32[12,18,7168]{2,0,1:T(8,128)}, f32[12,18,7168]{2,0,1:T(8,128)}) fusion(bf16[12,18,7168]{2,1,0:T(8,128)(2,1)} %param.4, f32[12,18,7168]{2,1,0:T(8,128)} %param.5, bf16[12,18,7168]{2,0,1:T(8,128)(2,1)} %collective-permute-done, pred[]{:T(512)S(6)} %eq.14), kind=kLoop, calls=%fused_computation.4 | loop fusion | flops 10838016 | bytes 24772608 | tf_op jit(solution)/shard_map/add | solution.py:61
  115.5 11.1 %pad_bitcast_fusion = f32[32,1,18,7168]{3,0,2,1:T(8,128)} fusion(f32[12,18,7168]{2,0,1:T(8,128)} %get-tuple-element.4), kind=kLoop, calls=%fused_computation.3 | loop fusion | bytes 22708224 | tf_op jit(solution)/shard_map/broadcast_in_dim | solution.py:65
  126.6 19.0 %copy.10 = f32[32,1,18,7168]{3,1,2,0:T(1,128)S(1)} copy(f32[32,1,18,7168]{3,0,2,1:T(8,128)} %pad_bitcast_fusion) | data formatting | bytes 33030144 | tf_op jit(solution)/shard_map/broadcast_in_dim | solution.py:65
  145.6 190.3 %all_to_all.21 = f32[32,1,18,7168]{3,1,2,0:T(1,128)S(1)} all-to-all(f32[32,1,18,7168]{3,1,2,0:T(1,128)S(1)} %copy.10), channel_id=1, replica_groups=mesh['zero'=32,'expert'=4] {'zero'}, dimensions={0} | all-to-all | bytes 33030144 | tf_op jit(solution)/shard_map/all_to_all | solution.py:66
  335.8 0.0 copy-start
  335.8 5.8 copy-done
  341.6 34.7 %multiply_reduce_fusion = f32[]{:T(128)} fusion(f32[32,1,18,7168]{3,1,2,0:T(1,128)S(1)} %all_to_all.21), kind=kLoop, calls=%fused_computation.2 | loop fusion | flops 8257535 | bytes 16515076 | tf_op jit(solution)/shard_map/reduce_sum | solution.py:67
  377.0 51.6 %divide_reduce_fusion = f32[32,18,7168]{2,1,0:T(8,128)} fusion(f32[32,1,18,7168]{3,1,2,0:T(1,128)} %copy-done, f32[]{:T(128)S(6)} %add.42), kind=kLoop, calls=%fused_computation | loop fusion | flops 4128768 | bytes 33030148 | tf_op jit(solution)/shard_map/div | solution.py:68
  428.6 15.1 %div.20 = f32[576,7168]{1,0:T(8,128)} reshape(f32[32,18,7168]{2,1,0:T(8,128)} %divide_reduce_fusion) | data formatting | bytes 33030144 | tf_op jit(solution)/shard_map/div | solution.py:68
  443.7 45.0 %fusion.18 = f32[576,576]{1,0:T(8,128)S(1)} fusion(f32[576,7168]{1,0:T(8,128)} %div.20), kind=kOutput, calls=%fused_computation.32 | convolution fusion | flops 28538044416 | bytes 17842176 | tf_op jit(solution)/shard_map/...ij,...kj->...ik/dot_general | solution.py:33
  488.7 4.3 fusion.2
  493.0 4.2 fusion.19
  497.2 2.0 fusion.9
  499.2 0.0 slice-start
  499.3 4.4 fusion.20
  503.7 0.0 slice-start.1
  503.7 4.2 fusion.3
  507.9 4.2 fusion.21
  512.2 0.0 slice-start.2
  512.2 4.7 fusion.24
  516.9 4.2 fusion.22
  521.1 0.0 slice-start.3
  521.1 4.2 fusion.23
  525.3 4.3 fusion.5
  529.6 0.0 slice-done
  529.6 0.0 slice-done.1
  529.6 0.0 slice-done.2
  529.6 0.0 slice-done.3
  529.6 44.3 %fusion = bf16[1,1,576,7168]{3,2,1,0:T(8,128)(2,1)S(1)} fusion(f32[576,576]{1,0:T(8,128)S(1)} %fusion.5, f32[576,7168]{1,0:T(8,128)S(1)} %bitcast.36), kind=kOutput, calls=%fused_computation.6 | convolution fusion | flops 28546301952 | bytes 26099712 | tf_op jit(solution)/shard_map/...ij,...jk->...ik/dot_general | solution.py:27
  573.9 37.1 %copy.27 = bf16[1,1,576,7168]{3,1,0,2:T(2,128)(2,1)} copy(bf16[1,1,576,7168]{3,2,1,0:T(8,128)(2,1)S(1)} %fusion) | data formatting | bytes 16515072 | tf_op jit(solution)/shard_map/convert_element_type | solution.py:70
  611.0 0.5 broadcast.68
  611.6 50.6 %reduce.5 = bf16[576,7168]{1,0:T(8,128)(2,1)} reduce(bf16[576,1,1,7168]{3,2,1,0:T(2,128)(2,1)} %bitcast.34, bf16[]{:T(256)} %broadcast.68), dimensions={1,2}, to_apply=%bitcast.33.reduce_sub_computation | reduce | bytes 16515074
  662.1 10.5 %reshape.106 = bf16[32,2,64512]{2,1,0:T(2,128)(2,1)} reshape(bf16[576,7168]{1,0:T(8,128)(2,1)} %reduce.5) | data formatting | bytes 16515072
  672.7 6.2 all-to-all-start.1
  678.8 10.4 %copy.12 = f32[12,18,7168]{2,1,0:T(8,128)} copy(f32[12,18,7168]{2,0,1:T(8,128)} %get-tuple-element.5) | data formatting | bytes 12386304
  689.2 111.0 %all-to-all-done.1 = bf16[32,2,64512]{2,1,0:T(2,128)(2,1)} async-done(((bf16[32,2,64512]{2,1,0:T(2,128)(2,1)}), bf16[32,2,64512]{2,1,0:T(2,128)(2,1)}, u32[]{:S(2)}, u32[]{:S(2)}) %all-to-all-start.1) | async-done | bytes 8257568 | tf_op jit(solution)/shard_map/all_to_all | solution.py:71
  800.2 23.0 %reshape.107 = bf16[576,1,1,7168]{3,2,1,0:T(2,128)(2,1)} reshape(bf16[32,2,64512]{2,1,0:T(2,128)(2,1)} %all-to-all-done.1) | data formatting | bytes 16515072
  823.2 52.5 %bitcast_reduce_fusion = bf16[576,7168]{1,0:T(8,128)(2,1)} fusion(bf16[576,1,1,7168]{3,2,1,0:T(2,128)(2,1)} %reshape.107), kind=kLoop, calls=%fused_computation.30 | loop fusion | bytes 16515072 | tf_op jit(solution)/shard_map/all_to_all | solution.py:71
  875.7 10.4 %all_to_all.8 = bf16[1,1,32,18,7168]{4,3,2,1,0:T(8,128)(2,1)} reshape(bf16[576,7168]{1,0:T(8,128)(2,1)} %bitcast_reduce_fusion) | data formatting | bytes 16515072 | tf_op jit(solution)/shard_map/all_to_all | solution.py:71
  886.1 4.4 slice_bitcast_fusion
  (1 shorter events, 0.0 us)
Async XLA Ops:
  0.6 10.0 %copy-start.1 = (s32[4]{0:T(128)S(1)}, s32[4]{0:T(128)}, u32[]{:S(2)}) copy-start(s32[4]{0:T(128)} %param.7) | copy-start | bytes 52
  9.3 91.7 %collective-permute-start = (bf16[12,18,7168]{2,0,1:T(8,128)(2,1)}, bf16[12,18,7168]{2,0,1:T(8,128)(2,1)}, u32[]{:S(2)}, u32[]{:S(2)}) collective-permute-start(bf16[12,18,7168]{2,0,1:T(8,128)(2,1)} %copy.23), channel_id=1, source_target_pairs={{0,1},{1,2},{2,3},{3,0},{4,5},{5,6},{6,7},{7,4},{8,9},{9,10},{10,1... | collective-permute-start | bytes 9289736 | tf_op jit(solution)/shard_map/ppermute | solution.py:23
  335.8 5.8 copy-start
  499.2 30.4 %slice-start = ((s8[16515072]{0:T(1024)(128)(4,1)}), s8[4194304]{0:T(1024)(128)(4,1)S(1)}, s32[]{:S(2)}) async-start(s8[16515072]{0:T(1024)(128)(4,1)} %bitcast.35), calls=%async_computation.2 | async-start | bytes 8388608
  503.7 25.9 %slice-start.1 = ((s8[16515072]{0:T(1024)(128)(4,1)}), s8[4194304]{0:T(1024)(128)(4,1)S(1)}, s32[]{:S(2)}) async-start(s8[16515072]{0:T(1024)(128)(4,1)} %bitcast.35), calls=%async_computation.3 | async-start | bytes 8388608
  512.2 17.4 %slice-start.2 = ((s8[16515072]{0:T(1024)(128)(4,1)}), s8[4194304]{0:T(1024)(128)(4,1)S(1)}, s32[]{:S(2)}) async-start(s8[16515072]{0:T(1024)(128)(4,1)} %bitcast.35), calls=%async_computation.4 | async-start | bytes 8388608
  521.1 8.5 slice-start.3
  672.7 127.5 %all-to-all-start.1 = ((bf16[32,2,64512]{2,1,0:T(2,128)(2,1)}), bf16[32,2,64512]{2,1,0:T(2,128)(2,1)}, u32[]{:S(2)}, u32[]{:S(2)}) async-start(bf16[32,2,64512]{2,1,0:T(2,128)(2,1)} %reshape.106), calls=%async_computation.1 | async-start | bytes 16515072 | tf_op jit(solution)/shard_map/all_to_all | solution.py:71
where the time goes:
time: 900 us; the launch traced here: 891 us
  local copies, waits for them, and re-layouts  209 us (23%)
  waiting for transfers between devices  200 us (22%)
  blocking collectives  190 us (21%)
  other arithmetic  151 us (17%)
  matrix products  130 us (14%)
    all_to_all x1, blocking collectives, local(): lax.all_to_all(parcel, 'zero', split_axis=0, concat_axis=2, tiled=True)  190 us
    all_to_all x1, waiting for transfers between devices, local(): lax.all_to_all(result, 'zero', split_axis=2, concat_axis=0, tiled=True)  111 us
    ppermute x1, waiting for transfers between devices, shifted(): return lax.ppermute(value, axis, pairs)  89.2 us
    dot_general x11, matrix products, mult(): jnp.einsum('...ij,...jk->...ik', left, right, precision=highest, preferre...  85.1 us
    all_to_all x2, local copies, waits for them, and re-layouts, local(): lax.all_to_all(result, 'zero', split_axis=2, concat_axis=0, tiled=True)  62.9 us
    unnamed x17, local copies, waits for them, and re-layouts  58.9 us
    div x1, other arithmetic, local(): start = held / (norm + eps)  51.6 us
    unnamed x2, other arithmetic  50.6 us
  transfers between devices with their start and end apart: 2, of which 2 were waited for; matrix products, arithmetic and copies ran while one was open for 1% of the time, Pallas kernels for 0%

commit v1 on v0

v1 whole, which is shorter than its diff:
```python
import jax
import jax.numpy as jnp
from jax import lax
from jax.experimental import pallas as pl
from jax.experimental.pallas import tpu as pltpu
from jax.sharding import PartitionSpec as P

MODEL_WIDTH = 7168
R = 576
MATS_GRP = 12
ROWS_DEV = 18
N_ZERO = 32
N_EXPERT = 4

beta = 0.95
coef_a = 3.4445
coef_b = -4.775
coef_c = 2.0315
eps = 1e-07
SCALE = 0.2 * max(R, MODEL_WIDTH) ** 0.5

CHUNKS = 8
CHUNK = MODEL_WIDTH // CHUNKS
PIECES = CHUNK // 128
UNIT = CHUNK + 128
MAIN = 16 * N_ZERO
HALF = R // 2

OWNER_CHIP = (0, 2, 5, 3, 11, 6, 4, 12, 9, 13, 15, 10)
HUB_CHIP = (1, 7, 8, 14)
TEAM_OF = (0, 0, 0, 1, 2, 0, 1, 1, 2, 2, 3, 1, 2, 3, 3, 3)
SPOT_OF = (0, 3, 1, 0, 0, 2, 2, 3, 3, 2, 2, 1, 1, 0, 3, 1)

STEPS = ((0, 0), (1, 0), (0, 1), (3, 0), (0, 3), (2, 0), (0, 2), (1, 1),
         (3, 3), (1, 3), (3, 1), (2, 1), (1, 2), (2, 3), (3, 2), (2, 2))

MESH = pl.DeviceIdType.MESH
f32 = jnp.float32
bf16 = jnp.bfloat16


def lut(index, table):
    value = jnp.int32(table[0])
    for place, entry in enumerate(table):
        if place:
            value = jnp.where(index == place, jnp.int32(entry), value)
    return value


def pack_rest(rest):
    pieces = [rest[:, 128 * g : 128 * (g + 1)] for g in range(PIECES)]
    return jnp.concatenate(pieces + [jnp.zeros((2, 128), rest.dtype)], axis=0)


def unpack_rest(tile):
    return jnp.concatenate([tile[2 * g : 2 * g + 2] for g in range(PIECES)], axis=1)


def times(left, right):
    return jnp.dot(left, right, preferred_element_type=f32)


def main_kernel(
    flags, grad, mom, back, out_ref, live_ref,
    gv, mv, bv, own, other, joined, shifted, units, x, o, perm, gram, gsend, gpeer, ghalf, gin, q,
    ma, mb, mc, md,
    in_sem, d_send, d_recv, y_send, y_recv, f_send, f_recv, a_send, a_recv, v_sem,
    g_send, g_recv, h_send, h_recv, k_send, k_recv, q_send, q_recv, p_send, p_recv, o_send, o_recv,
):
    zero, expert = lax.axis_index("zero"), lax.axis_index("expert")
    core = lax.rem(zero, 2)
    chip = zero // 2
    cx, cz = chip // 4, lax.rem(chip, 4)
    team, spot = lut(chip, TEAM_OF), lut(chip, SPOT_OF)
    is_owner = spot < 3
    is_hub = spot == 3
    twin = zero + 1 - 2 * core
    up = lax.rem(expert + 1, N_EXPERT)
    down = lax.rem(expert + N_EXPERT - 1, N_EXPERT)
    mine = pl.ds(4 * core, 4)
    theirs = pl.ds(4 - 4 * core, 4)
    lost = flags[0]
    mirror = flags[1]

    barrier = pltpu.get_barrier_semaphore()

    def greet(i, carry):
        pl.semaphore_signal(
            barrier, inc=1, device_id=(lax.rem(zero + i, N_ZERO), expert), device_id_type=MESH)
        return carry

    lax.fori_loop(1, N_ZERO, greet, 0)
    pl.semaphore_signal(barrier, inc=1, device_id=(zero, up), device_id_type=MESH)
    pl.semaphore_signal(barrier, inc=1, device_id=(zero, down), device_id_type=MESH)

    def matrix_at(i):
        return lax.rem(i + chip, MATS_GRP)

    def load(i, carry):
        m = matrix_at(i)
        pltpu.make_async_copy(back.at[m], bv.at[m], in_sem.at[0, m]).start()
        pltpu.make_async_copy(grad.at[m], gv.at[m], in_sem.at[1, m]).start()
        pltpu.make_async_copy(mom.at[m], mv.at[m], in_sem.at[2, m]).start()
        return carry

    lax.fori_loop(0, MATS_GRP, load, 0)

    rows = lax.broadcasted_iota(jnp.int32, (MAIN, MAIN), 0)
    cols = lax.broadcasted_iota(jnp.int32, (MAIN, MAIN), 1)
    wanted = 16 * (lax.rem(rows, 64) // 2) + 2 * (rows // 64) + lax.rem(rows, 2)
    perm[...] = jnp.where(cols == wanted, 1.0, 0.0).astype(bf16)

    pl.semaphore_wait(barrier, N_ZERO + 1)

    def to_twin(m):
        return pltpu.make_async_remote_copy(
            own.at[m, theirs], other.at[m], d_send.at[m], d_recv.at[m],
            device_id=(twin, expert), device_id_type=MESH)

    def to_up(m):
        return pltpu.make_async_remote_copy(
            joined.at[m], shifted.at[m, mine], y_send.at[m], y_recv.at[m],
            device_id=(zero, up), device_id_type=MESH)

    def forward(m):
        return pltpu.make_async_remote_copy(
            shifted.at[m, mine], shifted.at[m, mine], f_send.at[m], f_recv.at[m],
            device_id=(twin, expert), device_id_type=MESH)

    def forwarded(m):
        return pltpu.make_async_remote_copy(
            shifted.at[m, theirs], shifted.at[m, theirs], f_send.at[m], f_recv.at[m],
            device_id=(twin, expert), device_id_type=MESH)

    def keep(m):
        return pltpu.make_async_copy(shifted.at[m], live_ref.at[m], v_sem.at[m])

    def deliver(source, place, target):
        @pl.when(target != zero)
        def _():
            pltpu.make_async_remote_copy(
                source, place, a_send, a_recv, device_id=(target, expert), device_id_type=MESH).start()

        @pl.when(target == zero)
        def _():
            pltpu.make_async_copy(source, place, a_recv).start()

    my_rows = pl.ds(16 * zero, 16)

    def stage(i, carry):
        @pl.when(i < MATS_GRP)
        def _():
            m = matrix_at(i)
            pltpu.make_async_copy(back.at[m], bv.at[m], in_sem.at[0, m]).wait()
            for k in range(CHUNKS):
                span = pl.ds(CHUNK * k, CHUNK)
                own[m, k, :, :CHUNK] = (bv[m, :16, span] * mirror).astype(bf16)
                own[m, k, :, CHUNK:] = pack_rest(bv[m, 16:, span] * mirror).astype(bf16)
            to_twin(m).start()

        @pl.when(jnp.logical_and(i >= 1, i < MATS_GRP + 1))
        def _():
            m = matrix_at(i - 1)
            to_twin(m).wait_recv()
            joined[m] = own[m, mine] + other[m]
            to_up(m).start()

        @pl.when(jnp.logical_and(i >= 2, i < MATS_GRP + 2))
        def _():
            m = matrix_at(i - 2)
            to_up(m).wait_recv()
            forward(m).start()

        @pl.when(i >= 3)
        def _():
            m = matrix_at(i - 3)
            forwarded(m).wait_recv()
            keep(m).start()
            pltpu.make_async_copy(grad.at[m], gv.at[m], in_sem.at[1, m]).wait()
            pltpu.make_async_copy(mom.at[m], mv.at[m], in_sem.at[2, m]).wait()
            stale = (beta * beta) * (1.0 - lost)
            fresh = (beta * beta) * lost
            for k in range(CHUNKS):
                span = pl.ds(CHUNK * k, CHUNK)
                top = (1.0 + beta) * gv[m, :16, span].astype(f32) + stale * mv[m, :16, span]
                units[m, k, :, :CHUNK] = (
                    top + fresh * shifted[m, k, :, :CHUNK].astype(f32)).astype(bf16)
                rest = (1.0 + beta) * gv[m, 16:, span].astype(f32) + stale * mv[m, 16:, span]
                units[m, k, :, CHUNK:] = (
                    pack_rest(rest) + fresh * shifted[m, k, :, CHUNK:].astype(f32)).astype(bf16)
            hub, j, owner = lut(m // 3, HUB_CHIP), lax.rem(m, 3), lut(m, OWNER_CHIP)
            for c in range(2):
                deliver(units.at[m, pl.ds(6 + c, 1)], x.at[pl.ds(j, 1), my_rows], 2 * hub + c)
            for c in range(2):
                deliver(units.at[m, pl.ds(3 * c, 3)], x.at[:, my_rows], 2 * owner + c)
        return carry

    lax.fori_loop(0, MATS_GRP + 3, stage, 0)

    pltpu.make_async_copy(x.at[:, pl.ds(0, MAIN)], x.at[:, pl.ds(0, MAIN)], a_recv).wait()

    packed = jnp.concatenate([x[s, :MAIN, CHUNK:] for s in range(3)], axis=1)
    rest = times(perm[...], packed).astype(bf16)
    for s in range(3):
        for g in range(PIECES):
            x[s, MAIN:, 128 * g : 128 * (g + 1)] = rest[64 * g : 64 * (g + 1), 128 * s : 128 * (s + 1)]

    for s in range(3):
        block = x[s, :, :CHUNK]
        gram[s] = lax.dot_general(block, block, (((1,), (1,)), ((), ())), preferred_element_type=f32)

    my_half = pl.ds(HALF * core, HALF)
    their_half = pl.ds(HALF - HALF * core, HALF)

    def hub_to_twin():
        return pltpu.make_async_remote_copy(
            gsend.at[:, their_half], ghalf, h_send, h_recv,
            device_id=(twin, expert), device_id_type=MESH)

    def hub_to_owner(s):
        return pltpu.make_async_remote_copy(
            ghalf.at[s], gin.at[my_half], k_send.at[s], k_recv,
            device_id=(2 * lut(3 * team + s, OWNER_CHIP) + core, expert), device_id_type=MESH)

    def gram_to_twin():
        return pltpu.make_async_remote_copy(
            gram.at[0], gpeer, g_send, g_recv, device_id=(twin, expert), device_id_type=MESH)

    def half_to_twin():
        return pltpu.make_async_remote_copy(
            gin.at[my_half], gin.at[my_half], q_send.at[0], q_recv.at[0],
            device_id=(twin, expert), device_id_type=MESH)

    def poly_to_hub():
        return pltpu.make_async_remote_copy(
            q.at[0, my_half], q.at[spot, my_half], p_send.at[0], p_recv.at[spot],
            device_id=(2 * lut(team, HUB_CHIP) + core, expert), device_id_type=MESH)

    def poly_here(s):
        return pltpu.make_async_copy(q.at[s, my_half], q.at[s, my_half], p_recv.at[s])

    def poly_to_twin(s):
        return pltpu.make_async_remote_copy(
            q.at[s, my_half], q.at[s, my_half], q_send.at[s], q_recv.at[s],
            device_id=(twin, expert), device_id_type=MESH)

    @pl.when(is_hub)
    def _():
        for s in range(3):
            gsend[s] = gram[s].astype(bf16)
        hub_to_twin().start()
        hub_to_twin().wait_recv()
        for s in range(3):
            ghalf[s] = (gram[s, my_half] + ghalf[s].astype(f32)).astype(bf16)
            hub_to_owner(s).start()
        hub_to_twin().wait_send()
        for s in range(3):
            poly_here(s).wait()
            poly_to_twin(s).start()
        for s in range(3):
            hub_to_owner(s).wait_send()
            poly_to_twin(s).wait()

    @pl.when(is_owner)
    def _():
        gram[0] = gram[0] + gram[1] + gram[2]
        gram_to_twin().start()
        pltpu.make_async_copy(gin.at[my_half], gin.at[my_half], k_recv).wait()
        half_to_twin().start()
        gram_to_twin().wait()
        total = gram[0] + gpeer[...]
        half_to_twin().wait()
        total = total + gin[...].astype(f32)
        eye = (lax.broadcasted_iota(jnp.int32, (R, R), 0)
               == lax.broadcasted_iota(jnp.int32, (R, R), 1))
        norm = jnp.sqrt(jnp.sum(jnp.where(eye, total, 0.0)))
        inverse = 1.0 / (norm + eps)
        a, b, c = coef_a, coef_b, coef_c
        ga = total * (inverse * inverse)
        ma[...] = ga.astype(bf16)
        gram[0] = ga
        d1 = b * gram[0] + c * times(ma[...], ma[...])
        gram[1] = d1
        mb[...] = d1.astype(bf16)
        mc[...] = (2.0 * a * gram[1] + times(mb[...], mb[...])).astype(bf16)
        a1 = a * a * gram[0] + times(ma[...], mc[...])
        gram[0] = a1
        ma[...] = a1.astype(bf16)
        d2 = b * gram[0] + c * times(ma[...], ma[...])
        gram[2] = d2
        mc[...] = d2.astype(bf16)
        gram[1] = a * (gram[1] + gram[2]) + times(mb[...], mc[...])
        md[...] = (2.0 * a * gram[2] + times(mc[...], mc[...])).astype(bf16)
        a2 = a * a * gram[0] + times(ma[...], md[...])
        gram[0] = a2
        ma[...] = a2.astype(bf16)
        d3 = b * gram[0] + c * times(ma[...], ma[...])
        gram[2] = d3
        mb[...] = d3.astype(bf16)
        mc[...] = gram[1].astype(bf16)
        poly = a * gram[1] + a * a * gram[2] + times(mc[...], mb[...])
        poly = jnp.where(eye, poly + a * a * a, poly)
        q[0] = (poly * (inverse * SCALE)).astype(bf16)
        poly_to_hub().start()

    def outgoing(s, target):
        m = 3 * team + jnp.where(is_owner, spot, s)
        k = jnp.where(is_owner, 3 * core + s, 6 + core)
        source = o.at[s, pl.ds(16 * target, 16)]
        return source, out_ref.at[m, k]

    def spread(s, carry):
        which = jnp.where(is_owner, 0, s)
        block = x[s, :, :CHUNK]
        result = times(q[which], block).astype(bf16)
        o[s, :MAIN, :CHUNK] = result[:MAIN]
        stacked = jnp.concatenate(
            [result[MAIN:, 128 * g : 128 * (g + 1)] for g in range(PIECES)]
            + [jnp.zeros((64, 128), bf16)], axis=0)
        o[s, :MAIN, CHUNK:] = lax.dot_general(
            perm[...], stacked, (((0,), (0,)), ((), ())), preferred_element_type=f32).astype(bf16)

        def give(i, carry):
            place, other_core = lax.rem(i, 16), i // 16
            tx = lax.rem(cx + lut(place, [v[0] for v in STEPS]), 4)
            tz = lax.rem(cz + lut(place, [v[1] for v in STEPS]), 4)
            target = 8 * tx + 2 * tz + lax.rem(core + other_core, 2)
            source, dest = outgoing(s, target)
            pltpu.make_async_remote_copy(
                source, dest, o_send, o_recv, device_id=(target, expert), device_id_type=MESH).start()
            return carry

        lax.fori_loop(1, N_ZERO, give, 0)
        source, dest = outgoing(s, zero)
        pltpu.make_async_copy(source, dest, o_recv).start()
        return carry

    lax.fori_loop(0, 3, spread, 0)

    def drain(m, carry):
        to_twin(m).wait_send()
        to_up(m).wait_send()
        forward(m).wait_send()
        keep(m).wait()
        return carry

    lax.fori_loop(0, MATS_GRP, drain, 0)

    @pl.when(is_owner)
    def _():
        poly_to_hub().wait_send()

    sent = x.at[:, pl.ds(0, 16 * (N_ZERO - 1))]
    pltpu.make_async_copy(sent, sent, a_send).wait()
    pltpu.make_async_copy(sent, sent, o_send).wait()
    pltpu.make_async_copy(out_ref, out_ref, o_recv).wait()


def end_kernel(flags, back, live, grad, mom, new_ref, update_ref):
    lost = flags[0]
    stale = beta * (1.0 - lost)
    fresh = beta * lost
    for k in range(CHUNKS):
        span = pl.ds(CHUNK * k, CHUNK)
        update_ref[0, :16, span] = back[0, k, :, :CHUNK]
        update_ref[0, 16:, span] = unpack_rest(back[0, k, :, CHUNK:].astype(f32)).astype(bf16)
        new_ref[0, :16, span] = (
            grad[0, :16, span].astype(f32) + stale * mom[0, :16, span]
            + fresh * live[0, k, :, :CHUNK].astype(f32))
        new_ref[0, 16:, span] = (
            grad[0, 16:, span].astype(f32) + stale * mom[0, 16:, span]
            + fresh * unpack_rest(live[0, k, :, CHUNK:].astype(f32)))


def local(grad, momentum, backup, recovery):
    zero, expert = lax.axis_index("zero"), lax.axis_index("expert")
    lost = zero == recovery[expert]
    mirror = zero == recovery[lax.rem(expert + 1, N_EXPERT)]
    flags = jnp.stack([lost, mirror]).astype(f32)
    whole = (MATS_GRP, CHUNKS, 16, UNIT)
    halves = (MATS_GRP, CHUNKS // 2, 16, UNIT)
    shard = (MATS_GRP, ROWS_DEV, MODEL_WIDTH)
    anywhere = pl.BlockSpec(memory_space=pl.ANY)
    scalars = pl.BlockSpec(memory_space=pltpu.SMEM)
    dma = pltpu.SemaphoreType.DMA
    returned, live = pl.pallas_call(
        main_kernel,
        out_shape=[jax.ShapeDtypeStruct(whole, bf16)] * 2,
        in_specs=[scalars] + [anywhere] * 3,
        out_specs=[anywhere] * 2,
        scratch_shapes=[
            pltpu.VMEM(shard, bf16), pltpu.VMEM(shard, f32), pltpu.VMEM(shard, f32),
            pltpu.VMEM(whole, bf16), pltpu.VMEM(halves, bf16), pltpu.VMEM(halves, bf16),
            pltpu.VMEM(whole, bf16), pltpu.VMEM(whole, bf16),
            pltpu.VMEM((3, R, UNIT), bf16), pltpu.VMEM((3, MAIN, UNIT), bf16),
            pltpu.VMEM((MAIN, MAIN), bf16),
            pltpu.VMEM((3, R, R), f32), pltpu.VMEM((3, R, R), bf16), pltpu.VMEM((R, R), f32),
            pltpu.VMEM((3, HALF, R), bf16), pltpu.VMEM((R, R), bf16), pltpu.VMEM((3, R, R), bf16),
            pltpu.VMEM((R, R), bf16), pltpu.VMEM((R, R), bf16),
            pltpu.VMEM((R, R), bf16), pltpu.VMEM((R, R), bf16),
            dma((3, MATS_GRP)), dma((MATS_GRP,)), dma((MATS_GRP,)), dma((MATS_GRP,)),
            dma((MATS_GRP,)), dma((MATS_GRP,)), dma((MATS_GRP,)), dma, dma, dma((MATS_GRP,)),
            dma, dma, dma, dma, dma((3,)), dma, dma((3,)), dma((3,)), dma((1,)), dma((3,)), dma, dma,
        ],
        compiler_params=pltpu.CompilerParams(
            collective_id=0, has_side_effects=True, vmem_limit_bytes=60 << 20),
    )(flags, grad, momentum, backup)

    def unit_spec():
        return pl.BlockSpec((1, CHUNKS, 16, UNIT), lambda m: (m, 0, 0, 0))

    def shard_spec():
        return pl.BlockSpec((1, ROWS_DEV, MODEL_WIDTH), lambda m: (m, 0, 0))

    return pl.pallas_call(
        end_kernel,
        grid=(MATS_GRP,),
        out_shape=[jax.ShapeDtypeStruct(shard, f32), jax.ShapeDtypeStruct(shard, bf16)],
        in_specs=[scalars, unit_spec(), unit_spec(), shard_spec(), shard_spec()],
        out_specs=[shard_spec(), shard_spec()],
        compiler_params=pltpu.CompilerParams(vmem_limit_bytes=40 << 20),
    )(flags, returned, live, grad, momentum)


def solution(mesh):
    spread = P("expert", "zero", None)
    return jax.shard_map(
        local, mesh=mesh, in_specs=(spread, spread, spread, P()), out_specs=(spread, spread),
        check_vma=False)
```

time: 900 us -> 179 us (0.20)
  the two profiles are of different devices: /device:TPU:33 before, /device:TPU:3 now
where the time goes in v1:
time: 179 us
  Pallas kernels  171 us (96%)
  local copies, waits for them, and re-layouts  5.75 us (3%)
  between operations  1.97 us (1%)
    pallas_call x1, Pallas kernels, local(): pl.pallas_call(main_kernel, out_shape=[jax.ShapeDtypeStruct(whole, bf16)]...  159 us
    pallas_call x1, Pallas kernels, local(): pl.pallas_call(end_kernel, grid=(MATS_GRP,), out_shape=[jax.ShapeDtypeStr...  11.9 us
    unnamed x8, local copies, waits for them, and re-layouts  4.43 us

profile of v1, /device:TPU:3, one launch (start us, length us, event | category | flops | bytes accessed | tf_op | source)
XLA Modules:
  0.0 178.8 jit_solution(2096771300663744062)
XLA Ops:
  0.6 1.3 fusion
  3.3 0.6 add_convert_fusion.flags
  3.9 0.0 copy-start
  3.9 158.7 %shard_map.59 = (bf16[12,8,16,1024]{3,2,1,0:T(8,128)(2,1)}, bf16[12,8,16,1024]{3,2,1,0:T(8,128)(2,1)}) custom-call(f32[2]{0:T(128)} %add_convert_fusion.flags, bf16[12,18,7168]{2,1,0:T(8,128)(2,1)} %grad.3, f32[12,18,7168]{2,1,0:T(8,128)} %mom.3, f32[12,18,7168]{2,1,0:T(8,128)} %back.1), custom_call_target="tpu_custom_call" | custom-call | tf_op jit(solution)/shard_map/pallas_call | solution.py:386
  162.5 0.0 copy-done
  162.5 0.0 copy-start.1
  162.5 1.9 %copy-done.1 = bf16[12,8,16,1024]{3,2,1,0:T(8,128)(2,1)S(1)} copy-done((bf16[12,8,16,1024]{3,2,1,0:T(8,128)(2,1)S(1)}, bf16[12,8,16,1024]{3,2,1,0:T(8,128)(2,1)}, u32[]{:S(2)}) %copy-start.1) | copy-done | bytes 3145752
  164.4 0.0 copy-start.2
  164.4 1.9 %copy-done.2 = bf16[12,8,16,1024]{3,2,1,0:T(8,128)(2,1)S(1)} copy-done((bf16[12,8,16,1024]{3,2,1,0:T(8,128)(2,1)S(1)}, bf16[12,8,16,1024]{3,2,1,0:T(8,128)(2,1)}, u32[]{:S(2)}) %copy-start.2) | copy-done | bytes 3145752
  166.3 0.0 copy-start.3
  166.3 0.7 copy-done.3
  167.0 11.9 %shard_map.60 = (f32[12,18,7168]{2,1,0:T(8,128)}, bf16[12,18,7168]{2,1,0:T(8,128)(2,1)}) custom-call(f32[2]{0:T(128)S(1)} %copy-done.3, bf16[12,8,16,1024]{3,2,1,0:T(8,128)(2,1)S(1)} %copy-done.1, bf16[12,8,16,1024]{3,2,1,0:T(8,128)(2,1)S(1)} %copy-done.2, bf16[12,18,7168]{2,1,0:T(8,128)(2,1)S(1)} %copy-done, f32[12,18,7168]{2,1,0:T(8,128)} %mom.3), custom_call_target="tpu_custom_call" | custom-call | tf_op jit(solution)/shard_map/pallas_call | solution.py:415
Async XLA Ops:
  3.9 158.7 %copy-start = (bf16[12,18,7168]{2,1,0:T(8,128)(2,1)S(1)}, bf16[12,18,7168]{2,1,0:T(8,128)(2,1)}, u32[]{:S(2)}) copy-start(bf16[12,18,7168]{2,1,0:T(8,128)(2,1)} %grad.3) | copy-start | bytes 9289732
  162.5 1.9 %copy-start.1 = (bf16[12,8,16,1024]{3,2,1,0:T(8,128)(2,1)S(1)}, bf16[12,8,16,1024]{3,2,1,0:T(8,128)(2,1)}, u32[]{:S(2)}) copy-start(bf16[12,8,16,1024]{3,2,1,0:T(8,128)(2,1)} %get-tuple-element.4.back) | copy-start | bytes 9437188
  164.4 1.9 %copy-start.2 = (bf16[12,8,16,1024]{3,2,1,0:T(8,128)(2,1)S(1)}, bf16[12,8,16,1024]{3,2,1,0:T(8,128)(2,1)}, u32[]{:S(2)}) copy-start(bf16[12,8,16,1024]{3,2,1,0:T(8,128)(2,1)} %get-tuple-element.5.live) | copy-start | bytes 9437188
  166.3 0.7 copy-start.3

commit v2 on v1

v2 whole, which is shorter than its diff:
```python
import jax
import jax.numpy as jnp
from jax import lax
from jax.experimental import pallas as pl
from jax.experimental.pallas import tpu as pltpu
from jax.sharding import PartitionSpec as P

MODEL_WIDTH = 7168
R = 576
MATS_GRP = 12
ROWS_DEV = 18
N_ZERO = 32
N_EXPERT = 4

beta = 0.95
coef_a = 3.4445
coef_b = -4.775
coef_c = 2.0315
eps = 1e-07
SCALE = 0.2 * max(R, MODEL_WIDTH) ** 0.5

CHUNKS = 8
CHUNK = MODEL_WIDTH // CHUNKS
PIECES = CHUNK // 128
UNIT = CHUNK + 128
MAIN = 16 * N_ZERO
HALF = R // 2

CHIP_OF = (0, 2, 5, 1, 3, 11, 6, 7, 4, 12, 9, 8, 13, 15, 10, 14)
TARGET_OF = tuple(CHIP_OF.index(chip) for chip in range(16))
OWNED = 6 * CHUNK

STEPS = ((0, 0), (1, 0), (0, 1), (3, 0), (0, 3), (2, 0), (0, 2), (1, 1),
         (3, 3), (1, 3), (3, 1), (2, 1), (1, 2), (2, 3), (3, 2), (2, 2))
FAR_FIRST = STEPS[:0:-1] + STEPS[:1]
EVEN_STEPS = tuple(v for v in STEPS if sum(v) % 2 == 0)
ODD_STEPS = tuple(v for v in STEPS if sum(v) % 2 == 1)


def order_of(chip):
    x, z = chip // 4, chip % 4
    return [TARGET_OF[4 * ((x + dx) % 4) + (z + dz) % 4] for dx, dz in FAR_FIRST]


CODES = tuple(
    tuple(sum(order_of(chip)[4 * part + i] * 16 ** i for i in range(4)) for chip in range(16))
    for part in range(4))

JOIN, LIFT, SEND = 1, 3, 4

MESH = pl.DeviceIdType.MESH
f32 = jnp.float32
bf16 = jnp.bfloat16


def lut(index, table):
    value = jnp.int32(table[0])
    for place, entry in enumerate(table):
        if place:
            value = jnp.where(index == place, jnp.int32(entry), value)
    return value


def pack_rest(rest):
    pieces = [rest[:, 128 * g : 128 * (g + 1)] for g in range(PIECES)]
    return jnp.concatenate(pieces + [jnp.zeros((2, 128), rest.dtype)], axis=0)


def unpack_rest(tile):
    return jnp.concatenate([tile[2 * g : 2 * g + 2] for g in range(PIECES)], axis=1)


def times(left, right):
    return jnp.dot(left, right, preferred_element_type=f32)


def main_kernel(
    recovery, grad, mom, back, out_ref, live_ref, lost_ref,
    gv, mv, bv, own, other, joined, shifted, units, x, o, perm, gram, gsend, gpeer, ghalf, gin, q,
    ma, mb, mc, md,
    in_sem, d_send, d_recv, y_send, y_recv, f_send, f_recv, a_send, a_recv, v_sem,
    g_send, g_recv, h_send, h_recv, k_send, k_recv, i_send, i_recv, q_send, q_recv, p_send, p_recv,
    o_send, o_recv,
):
    zero, expert = lax.axis_index("zero"), lax.axis_index("expert")
    core = lax.rem(zero, 2)
    chip = zero // 2
    cx, cz = chip // 4, lax.rem(chip, 4)
    parity = lax.rem(cx + cz, 2)
    me = lut(chip, TARGET_OF)
    team, spot = me // 4, lax.rem(me, 4)
    is_owner = spot < 3
    is_hub = spot == 3
    twin = zero + 1 - 2 * core
    up = lax.rem(expert + 1, N_EXPERT)
    down = lax.rem(expert + N_EXPERT - 1, N_EXPERT)
    my_rows = pl.ds(16 * (16 * core + 8 * parity + 2 * cx + cz // 2), 16)
    lost = jnp.where(recovery[expert] == zero, 1.0, 0.0)
    mirror = jnp.where(recovery[up] == zero, 1.0, 0.0)
    lost_ref[0] = jnp.where(recovery[expert] == zero, 1, 0)

    barrier = pltpu.get_barrier_semaphore()

    def greet(i, carry):
        pl.semaphore_signal(
            barrier, inc=1, device_id=(lax.rem(zero + i, N_ZERO), expert), device_id_type=MESH)
        return carry

    lax.fori_loop(1, N_ZERO, greet, 0)
    pl.semaphore_signal(barrier, inc=1, device_id=(zero, up), device_id_type=MESH)
    pl.semaphore_signal(barrier, inc=1, device_id=(zero, down), device_id_type=MESH)

    codes = [lut(chip, table) for table in CODES]

    def next_target(i, code):
        fresh = jnp.where(
            i < 4, codes[0], jnp.where(i < 8, codes[1], jnp.where(i < 12, codes[2], codes[3])))
        code = jnp.where(lax.rem(i, 4) == 0, fresh, code // 16)
        return lax.rem(code, 16), code

    def loads(target, source, dest, sem, act):
        t, place = target // 4, lax.rem(target, 4)

        @pl.when(place < 3)
        def _():
            part = (3 * t + place, slice(None), pl.ds(0, OWNED))
            act(pltpu.make_async_copy(source.at[part], dest.at[part], sem))

        @pl.when(place == 3)
        def _():
            part = (pl.ds(3 * t, 3), slice(None), pl.ds(OWNED, MODEL_WIDTH - OWNED))
            act(pltpu.make_async_copy(source.at[part], dest.at[part], sem))

    def back_loads(target, act):
        loads(target, back, bv, in_sem.at[0, target], act)

    def grad_loads(target, act):
        loads(target, grad, gv, in_sem.at[1, target], act)

    def mom_loads(target, act):
        loads(target, mom, mv, in_sem.at[2, target], act)

    def begin(copy):
        copy.start()

    def finish(copy):
        copy.wait()

    def load(i, code):
        target, code = next_target(i, code)
        back_loads(target, begin)
        grad_loads(target, begin)
        mom_loads(target, begin)
        return code

    lax.fori_loop(0, 16, load, jnp.int32(0))

    def sources(target, u):
        t, place = target // 4, lax.rem(target, 4)
        c, s = u // 3, u % 3
        m = 3 * t + jnp.where(place < 3, place, s)
        k = jnp.where(place < 3, 3 * c + s, 6 + c)
        return c, s, m, pl.ds(pl.multiple_of(k * CHUNK, 128), CHUNK)

    def make_own(target):
        back_loads(target, finish)
        for u in range(6):
            c, s, m, span = sources(target, u)
            own[target, c, s, :, :CHUNK] = (bv[m, :16, span] * mirror).astype(bf16)
            own[target, c, s, :, CHUNK:] = pack_rest(bv[m, 16:, span] * mirror).astype(bf16)

    def make_units(target):
        grad_loads(target, finish)
        mom_loads(target, finish)
        stale = (beta * beta) * (1.0 - lost)
        fresh = (beta * beta) * lost
        for u in range(6):
            c, s, m, span = sources(target, u)
            top = (1.0 + beta) * gv[m, :16, span].astype(f32) + stale * mv[m, :16, span]
            units[target, c, s, :, :CHUNK] = (
                top + fresh * shifted[target, c, s, :, :CHUNK].astype(f32)).astype(bf16)
            rest = (1.0 + beta) * gv[m, 16:, span].astype(f32) + stale * mv[m, 16:, span]
            units[target, c, s, :, CHUNK:] = (
                pack_rest(rest) + fresh * shifted[target, c, s, :, CHUNK:].astype(f32)).astype(bf16)

    rows = lax.broadcasted_iota(jnp.int32, (MAIN, MAIN), 0)
    cols = lax.broadcasted_iota(jnp.int32, (MAIN, MAIN), 1)
    wanted = 16 * (lax.rem(rows, 64) // 2) + 2 * (rows // 64) + lax.rem(rows, 2)
    perm[...] = jnp.where(cols == wanted, 1.0, 0.0).astype(bf16)

    first, first_code = next_target(jnp.int32(0), jnp.int32(0))
    make_own(first)

    pl.semaphore_wait(barrier, N_ZERO + 1)

    def to_twin(n):
        return pltpu.make_async_remote_copy(
            own.at[n, 1 - core], other.at[n], d_send.at[n], d_recv.at[n],
            device_id=(twin, expert), device_id_type=MESH)

    def to_up(n):
        return pltpu.make_async_remote_copy(
            joined.at[n], shifted.at[n, core], y_send.at[n], y_recv.at[n],
            device_id=(zero, up), device_id_type=MESH)

    def forward(n):
        return pltpu.make_async_remote_copy(
            shifted.at[n, core], shifted.at[n, core], f_send.at[n], f_recv.at[n],
            device_id=(twin, expert), device_id_type=MESH)

    def keep(n):
        return pltpu.make_async_copy(shifted.at[n], live_ref.at[n], v_sem.at[n])

    def deliver(source, target):
        place = x.at[:, my_rows]

        @pl.when(target != zero)
        def _():
            pltpu.make_async_remote_copy(
                source, place, a_send, a_recv, device_id=(target, expert), device_id_type=MESH).start()

        @pl.when(target == zero)
        def _():
            pltpu.make_async_copy(source, place, a_recv).start()

    def gather_rest():
        pltpu.make_async_copy(x.at[:, pl.ds(0, MAIN)], x.at[:, pl.ds(0, MAIN)], a_recv).wait()
        packed = jnp.concatenate([x[s, :MAIN, CHUNK:] for s in range(3)], axis=1)
        rest = times(perm[...], packed).astype(bf16)
        for s in range(3):
            for g in range(PIECES):
                x[s, MAIN:, 128 * g : 128 * (g + 1)] = (
                    rest[64 * g : 64 * (g + 1), 128 * s : 128 * (s + 1)])

    def gram_of(s):
        block = x[s, :, :CHUNK]
        return lax.dot_general(block, block, (((1,), (1,)), ((), ())), preferred_element_type=f32)

    my_half = pl.ds(HALF * core, HALF)
    their_half = pl.ds(HALF - HALF * core, HALF)

    def hub_to_twin(s):
        return pltpu.make_async_remote_copy(
            gsend.at[s, their_half], ghalf.at[s], h_send.at[s], h_recv.at[s],
            device_id=(twin, expert), device_id_type=MESH)

    def hub_to_owner(s):
        return pltpu.make_async_remote_copy(
            ghalf.at[s], gin.at[my_half], k_send.at[s], k_recv,
            device_id=(2 * lut(4 * team + s, CHIP_OF) + core, expert), device_id_type=MESH)

    def stage(i, carry):
        code, past = carry[0], carry[1:]
        now = past[0]

        @pl.when(i < 16)
        def _():
            to_twin(now).start()

        @pl.when(jnp.logical_and(i >= JOIN, i < 16 + JOIN))
        def _():
            to_twin(past[JOIN]).wait_recv()
            joined[past[JOIN]] = own[past[JOIN], core] + other[past[JOIN]]
            to_up(past[JOIN]).start()

        @pl.when(jnp.logical_and(i >= LIFT, i < 16 + LIFT))
        def _():
            to_up(past[LIFT]).wait_recv()
            forward(past[LIFT]).start()

        @pl.when(i >= SEND)
        def _():
            forward(past[SEND]).wait_recv()
            keep(past[SEND]).start()
            make_units(past[SEND])
            for c in range(2):
                deliver(units.at[past[SEND], c], 2 * lut(past[SEND], CHIP_OF) + c)

        later, code = next_target(i + 1, code)

        @pl.when(i + 1 < 16)
        def _():
            make_own(later)

        return (code, later) + past[:SEND]

    lax.fori_loop(0, 16 + SEND, stage, (first_code, first) + (jnp.int32(0),) * SEND)

    def gram_to_twin():
        return pltpu.make_async_remote_copy(
            gram.at[0], gpeer, g_send, g_recv, device_id=(twin, expert), device_id_type=MESH)

    def half_to_twin():
        return pltpu.make_async_remote_copy(
            gin.at[my_half], gin.at[my_half], i_send, i_recv,
            device_id=(twin, expert), device_id_type=MESH)

    def part_rows(n):
        return pl.ds(MAIN + 32 * core, 32) if n == 0 else pl.ds(128 * (n - 1) + 64 * core, 64)

    def poly_to_hub(n):
        return pltpu.make_async_remote_copy(
            q.at[0, part_rows(n)], q.at[spot, part_rows(n)], p_send.at[n], p_recv.at[spot, n],
            device_id=(2 * lut(4 * team + 3, CHIP_OF) + core, expert), device_id_type=MESH)

    def poly_to_twin(s, n):
        return pltpu.make_async_remote_copy(
            q.at[s, part_rows(n)], q.at[s, part_rows(n)], q_send.at[s, n], q_recv.at[s, n],
            device_id=(twin, expert), device_id_type=MESH)

    gather_rest()

    @pl.when(is_hub)
    def _():
        for s in range(3):
            part = gram_of(s)
            gram[s] = part
            gsend[s] = part.astype(bf16)
            hub_to_twin(s).start()
        for s in range(3):
            hub_to_twin(s).wait_recv()
            ghalf[s] = (gram[s, my_half] + ghalf[s].astype(f32)).astype(bf16)
            hub_to_owner(s).start()

    @pl.when(is_owner)
    def _():
        gram[0] = gram_of(0) + gram_of(1) + gram_of(2)
        gram_to_twin().start()
        pltpu.make_async_copy(gin.at[my_half], gin.at[my_half], k_recv).wait()
        half_to_twin().start()
        gram_to_twin().wait()
        total = gram[0] + gpeer[...]
        half_to_twin().wait()
        total = total + gin[...].astype(f32)
        eye = (lax.broadcasted_iota(jnp.int32, (R, R), 0)
               == lax.broadcasted_iota(jnp.int32, (R, R), 1))
        norm = jnp.sqrt(jnp.sum(jnp.where(eye, total, 0.0)))
        inverse = 1.0 / (norm + eps)
        a, b, c = coef_a, coef_b, coef_c
        ga = total * (inverse * inverse)
        ma[...] = ga.astype(bf16)
        gram[0] = ga
        d1 = b * gram[0] + c * times(ma[...], ma[...])
        gram[1] = d1
        mb[...] = d1.astype(bf16)
        mc[...] = (2.0 * a * gram[1] + times(mb[...], mb[...])).astype(bf16)
        a1 = a * a * gram[0] + times(ma[...], mc[...])
        gram[0] = a1
        ma[...] = a1.astype(bf16)
        d2 = b * gram[0] + c * times(ma[...], ma[...])
        gram[2] = d2
        mc[...] = d2.astype(bf16)
        gram[1] = a * (gram[1] + gram[2]) + times(mb[...], mc[...])
        md[...] = (2.0 * a * gram[2] + times(mc[...], mc[...])).astype(bf16)
        a2 = a * a * gram[0] + times(ma[...], md[...])
        gram[0] = a2
        ma[...] = a2.astype(bf16)
        d3 = b * gram[0] + c * times(ma[...], ma[...])
        gram[2] = d3
        mb[...] = d3.astype(bf16)
        mc[...] = gram[1].astype(bf16)
        poly = a * gram[1] + a * a * gram[2] + times(mc[...], mb[...])
        poly = jnp.where(eye, poly + a * a * a, poly)
        q[0] = (poly * (inverse * SCALE)).astype(bf16)
        for n in range(5):
            poly_to_hub(n).start()

    def arrive(n):
        @pl.when(is_hub)
        def _():
            for s in range(3):
                pltpu.make_async_copy(
                    q.at[s, part_rows(n)], q.at[s, part_rows(n)], p_recv.at[s, n]).wait()
                poly_to_twin(s, n).start()
            for s in range(3):
                poly_to_twin(s, n).wait_recv()

    def apply(s, rows):
        which = jnp.where(is_owner, 0, s)
        return times(q[which, rows], x[s, :, :CHUNK]).astype(bf16)

    arrive(0)
    for s in range(3):
        rest = apply(s, pl.ds(MAIN, R - MAIN))
        stacked = jnp.concatenate(
            [rest[:, 128 * g : 128 * (g + 1)] for g in range(PIECES)]
            + [jnp.zeros((64, 128), bf16)], axis=0)
        o[s, :, CHUNK:] = lax.dot_general(
            perm[...], stacked, (((0,), (0,)), ((), ())), preferred_element_type=f32).astype(bf16)

    for n in range(4):
        arrive(n + 1)
        for s in range(3):
            o[s, 128 * n : 128 * (n + 1), :CHUNK] = apply(s, pl.ds(128 * n, 128))
        to_core, to_parity = n // 2, n % 2
        odd = parity != to_parity

        def give(i, carry):
            tx = lax.rem(cx + lut(jnp.where(odd, i + 8, i), [v[0] for v in EVEN_STEPS + ODD_STEPS]), 4)
            tz = lax.rem(cz + lut(jnp.where(odd, i + 8, i), [v[1] for v in EVEN_STEPS + ODD_STEPS]), 4)
            target = 8 * tx + 2 * tz + to_core
            source = o.at[:, pl.ds(128 * n + 16 * (2 * tx + tz // 2), 16)]

            @pl.when(target != zero)
            def _():
                pltpu.make_async_remote_copy(
                    source, out_ref.at[me, core], o_send, o_recv,
                    device_id=(target, expert), device_id_type=MESH).start()

            @pl.when(target == zero)
            def _():
                pltpu.make_async_copy(source, out_ref.at[me, core], o_recv).start()

            return carry

        lax.fori_loop(0, 8, give, 0)

    def drain(n, carry):
        to_twin(n).wait_send()
        to_up(n).wait_send()
        forward(n).wait_send()
        keep(n).wait()
        return carry

    lax.fori_loop(0, 16, drain, 0)

    @pl.when(is_owner)
    def _():
        for n in range(5):
            poly_to_hub(n).wait_send()

    @pl.when(is_hub)
    def _():
        for s in range(3):
            hub_to_twin(s).wait_send()
            hub_to_owner(s).wait_send()
            for n in range(5):
                poly_to_twin(s, n).wait_send()

    sent = x.at[:, pl.ds(0, 16 * (N_ZERO - 1))]
    pltpu.make_async_copy(sent, sent, a_send).wait()
    pltpu.make_async_copy(sent, sent, o_send).wait()
    pltpu.make_async_copy(out_ref, out_ref, o_recv).wait()


def end_kernel(lost_ref, back, back_hub, live, live_hub, grad, mom, new_ref, update_ref):
    lost = lost_ref[0].astype(f32)
    stale = beta * (1.0 - lost)
    fresh = beta * lost
    for k in range(CHUNKS):
        span = pl.ds(CHUNK * k, CHUNK)
        unit = (0, 0, k // 3, k % 3) if k < 6 else (0, 0, k - 6, 0)
        returned = back if k < 6 else back_hub
        held = live if k < 6 else live_hub
        update_ref[0, :16, span] = returned[unit][:, :CHUNK]
        update_ref[0, 16:, span] = unpack_rest(returned[unit][:, CHUNK:].astype(f32)).astype(bf16)
        new_ref[0, :16, span] = (
            grad[0, :16, span].astype(f32) + stale * mom[0, :16, span]
            + fresh * held[unit][:, :CHUNK].astype(f32))
        new_ref[0, 16:, span] = (
            grad[0, 16:, span].astype(f32) + stale * mom[0, 16:, span]
            + fresh * unpack_rest(held[unit][:, CHUNK:].astype(f32)))


def local(grad, momentum, backup, recovery):
    whole = (16, 2, 3, 16, UNIT)
    halves = (16, 3, 16, UNIT)
    shard = (MATS_GRP, ROWS_DEV, MODEL_WIDTH)
    anywhere = pl.BlockSpec(memory_space=pl.ANY)
    scalars = pl.BlockSpec(memory_space=pltpu.SMEM)
    dma = pltpu.SemaphoreType.DMA
    steps = dma((16,))
    returned, live, lost = pl.pallas_call(
        main_kernel,
        out_shape=[jax.ShapeDtypeStruct(whole, bf16)] * 2 + [jax.ShapeDtypeStruct((1,), jnp.int32)],
        in_specs=[scalars] + [anywhere] * 3,
        out_specs=[anywhere] * 2 + [scalars],
        scratch_shapes=[
            pltpu.VMEM(shard, bf16), pltpu.VMEM(shard, f32), pltpu.VMEM(shard, f32),
            pltpu.VMEM(whole, bf16), pltpu.VMEM(halves, bf16), pltpu.VMEM(halves, bf16),
            pltpu.VMEM(whole, bf16), pltpu.VMEM(whole, bf16),
            pltpu.VMEM((3, R, UNIT), bf16), pltpu.VMEM((3, MAIN, UNIT), bf16),
            pltpu.VMEM((MAIN, MAIN), bf16),
            pltpu.VMEM((3, R, R), f32), pltpu.VMEM((3, R, R), bf16), pltpu.VMEM((R, R), f32),
            pltpu.VMEM((3, HALF, R), bf16), pltpu.VMEM((R, R), bf16), pltpu.VMEM((3, R, R), bf16),
            pltpu.VMEM((R, R), bf16), pltpu.VMEM((R, R), bf16),
            pltpu.VMEM((R, R), bf16), pltpu.VMEM((R, R), bf16),
            dma((3, 16)), steps, steps, steps, steps, steps, steps, dma, dma, steps,
            dma, dma, dma((3,)), dma((3,)), dma((3,)), dma, dma, dma,
            dma((3, 5)), dma((3, 5)), dma((5,)), dma((3, 5)), dma, dma,
        ],
        compiler_params=pltpu.CompilerParams(
            collective_id=0, has_side_effects=True, vmem_limit_bytes=60 << 20),
    )(recovery, grad, momentum, backup)

    def owner_block(m, scale=1):
        return (m // 3 * scale, lax.rem(m, 3) * scale, 0, 0, 0, 0)

    def hub_block(m, scale=1):
        return (m // 3 * scale, 3, 0, lax.rem(m, 3) * scale, 0, 0)

    owner_shape, hub_shape = (1, 1, 2, 3, 16, UNIT), (1, 1, 2, 1, 16, UNIT)
    plain = pl.BlockSpec((1, ROWS_DEV, MODEL_WIDTH), lambda m, lost: (m, 0, 0))
    parted = (4, 4, 2, 3, 16, UNIT)
    return pl.pallas_call(
        end_kernel,
        grid_spec=pltpu.PrefetchScalarGridSpec(
            num_scalar_prefetch=1,
            grid=(MATS_GRP,),
            in_specs=[
                pl.BlockSpec(owner_shape, lambda m, lost: owner_block(m)),
                pl.BlockSpec(hub_shape, lambda m, lost: hub_block(m)),
                pl.BlockSpec(owner_shape, lambda m, lost: owner_block(m, lost[0])),
                pl.BlockSpec(hub_shape, lambda m, lost: hub_block(m, lost[0])),
                plain,
                pl.BlockSpec((1, ROWS_DEV, MODEL_WIDTH), lambda m, lost: (m * (1 - lost[0]), 0, 0)),
            ],
            out_specs=[plain, plain],
        ),
        out_shape=[jax.ShapeDtypeStruct(shard, f32), jax.ShapeDtypeStruct(shard, bf16)],
        compiler_params=pltpu.CompilerParams(vmem_limit_bytes=60 << 20),
    )(lost, returned.reshape(parted), returned.reshape(parted), live.reshape(parted),
      live.reshape(parted), grad, momentum)


def solution(mesh):
    spread = P("expert", "zero", None)
    return jax.shard_map(
        local, mesh=mesh, in_specs=(spread, spread, spread, P()), out_specs=(spread, spread),
        check_vma=False)
```

time: 179 us -> 150 us (0.84)
  the two profiles are of different devices: /device:TPU:3 before, /device:TPU:33 now
where the time goes in v2:
time: 150 us; the launch traced here: 149 us
  Pallas kernels  149 us (99%)
    pallas_call x1, Pallas kernels, local(): pl.pallas_call(main_kernel, out_shape=[jax.ShapeDtypeStruct(whole, bf16)]...  134 us
    pallas_call x1, Pallas kernels, local(): pl.pallas_call(end_kernel, grid_spec=pltpu.PrefetchScalarGridSpec(num_sca...  14.8 us

profile of v2, /device:TPU:33, one launch (start us, length us, event | category | flops | bytes accessed | tf_op | source)
XLA Modules:
  0.0 149.3 jit_solution(12457954574235914582)
XLA Ops:
  0.6 133.9 %shard_map.59 = (bf16[16,2,3,16,1024]{4,3,2,1,0:T(8,128)(2,1)}, bf16[16,2,3,16,1024]{4,3,2,1,0:T(8,128)(2,1)}, s32[1]{0:T(128)}) custom-call(s32[4]{0:T(128)} %recovery.1, bf16[12,18,7168]{2,1,0:T(8,128)(2,1)} %grad.3, f32[12,18,7168]{2,1,0:T(8,128)} %mom.3, f32[12,18,7168]{2,1,0:T(8,128)} %back.1), custom_call_target="tpu_custom_call" | custom-call | tf_op jit(solution)/shard_map/pallas_call | solution.py:473
  134.6 14.8 %shard_map.60 = (f32[12,18,7168]{2,1,0:T(8,128)}, bf16[12,18,7168]{2,1,0:T(8,128)(2,1)}) custom-call(s32[1]{0:T(128)} %get-tuple-element.5.lost_ref, bf16[4,4,2,3,16,1024]{5,4,3,2,1,0:T(8,128)(2,1)} %bitcast.2, bf16[4,4,2,3,16,1024]{5,4,3,2,1,0:T(8,128)(2,1)} %bitcast.3, bf16[4,4,2,3,16,1024]{5,4,3,2,1,0:T(8,128)(2,1)} %bitcast.4, ...), custom_call_target="tpu_custom_call" | custom-call | tf_op jit(solution)/shard_map/pallas_call | solution.py:505

commit v3 on v2

--- a/solution.py
+++ b/solution.py
@@ -35,11 +35,17 @@
 FAR_FIRST = STEPS[:0:-1] + STEPS[:1]
 EVEN_STEPS = tuple(v for v in STEPS if sum(v) % 2 == 0)
 ODD_STEPS = tuple(v for v in STEPS if sum(v) % 2 == 1)
+HUBS_BEFORE = 8
 
 
 def order_of(chip):
     x, z = chip // 4, chip % 4
-    return [TARGET_OF[4 * ((x + dx) % 4) + (z + dz) % 4] for dx, dz in FAR_FIRST]
+    turns = [TARGET_OF[4 * ((x + dx) % 4) + (z + dz) % 4] for dx, dz in FAR_FIRST]
+    for late in range(HUBS_BEFORE, 16):
+        if turns[late] % 4 == 3:
+            early = max(i for i in range(HUBS_BEFORE) if turns[i] % 4 != 3)
+            turns[late], turns[early] = turns[early], turns[late]
+    return turns
 
 
 CODES = tuple(
@@ -232,9 +238,9 @@
                 x[s, MAIN:, 128 * g : 128 * (g + 1)] = (
                     rest[64 * g : 64 * (g + 1), 128 * s : 128 * (s + 1)])
 
-    def gram_of(s):
-        block = x[s, :, :CHUNK]
-        return lax.dot_general(block, block, (((1,), (1,)), ((), ())), preferred_element_type=f32)
+    def gram_of(s, rows=slice(None)):
+        return lax.dot_general(
+            x[s, rows, :CHUNK], x[s, :, :CHUNK], (((1,), (1,)), ((), ())), preferred_element_type=f32)
 
     my_half = pl.ds(HALF * core, HALF)
     their_half = pl.ds(HALF - HALF * core, HALF)
@@ -248,6 +254,11 @@
         return pltpu.make_async_remote_copy(
             ghalf.at[s], gin.at[my_half], k_send.at[s], k_recv,
             device_id=(2 * lut(4 * team + s, CHIP_OF) + core, expert), device_id_type=MESH)
+
+    def pass_on(s):
+        hub_to_twin(s).wait_recv()
+        ghalf[s] = (gram[s, my_half] + ghalf[s].astype(f32)).astype(bf16)
+        hub_to_owner(s).start()
 
     def stage(i, carry):
         code, past = carry[0], carry[1:]
@@ -286,9 +297,11 @@
 
     lax.fori_loop(0, 16 + SEND, stage, (first_code, first) + (jnp.int32(0),) * SEND)
 
-    def gram_to_twin():
-        return pltpu.make_async_remote_copy(
-            gram.at[0], gpeer, g_send, g_recv, device_id=(twin, expert), device_id_type=MESH)
+    def gram_to_twin(n):
+        rows = pl.ds(HALF * n, HALF)
+        return pltpu.make_async_remote_copy(
+            gram.at[0, rows], gpeer.at[rows], g_send.at[n], g_recv.at[n],
+            device_id=(twin, expert), device_id_type=MESH)
 
     def half_to_twin():
         return pltpu.make_async_remote_copy(
@@ -317,18 +330,20 @@
             gram[s] = part
             gsend[s] = part.astype(bf16)
             hub_to_twin(s).start()
-        for s in range(3):
-            hub_to_twin(s).wait_recv()
-            ghalf[s] = (gram[s, my_half] + ghalf[s].astype(f32)).astype(bf16)
-            hub_to_owner(s).start()
+            if s:
+                pass_on(s - 1)
+        pass_on(2)
 
     @pl.when(is_owner)
     def _():
-        gram[0] = gram_of(0) + gram_of(1) + gram_of(2)
-        gram_to_twin().start()
+        for n in range(2):
+            rows = slice(HALF * n, HALF * (n + 1))
+            gram[0, rows] = gram_of(0, rows) + gram_of(1, rows) + gram_of(2, rows)
+            gram_to_twin(n).start()
         pltpu.make_async_copy(gin.at[my_half], gin.at[my_half], k_recv).wait()
         half_to_twin().start()
-        gram_to_twin().wait()
+        gram_to_twin(0).wait()
+        gram_to_twin(1).wait()
         total = gram[0] + gpeer[...]
         half_to_twin().wait()
         total = total + gin[...].astype(f32)
@@ -443,23 +458,89 @@
     pltpu.make_async_copy(out_ref, out_ref, o_recv).wait()
 
 
-def end_kernel(lost_ref, back, back_hub, live, live_hub, grad, mom, new_ref, update_ref):
-    lost = lost_ref[0].astype(f32)
-    stale = beta * (1.0 - lost)
-    fresh = beta * lost
-    for k in range(CHUNKS):
-        span = pl.ds(CHUNK * k, CHUNK)
-        unit = (0, 0, k // 3, k % 3) if k < 6 else (0, 0, k - 6, 0)
-        returned = back if k < 6 else back_hub
-        held = live if k < 6 else live_hub
-        update_ref[0, :16, span] = returned[unit][:, :CHUNK]
-        update_ref[0, 16:, span] = unpack_rest(returned[unit][:, CHUNK:].astype(f32)).astype(bf16)
-        new_ref[0, :16, span] = (
-            grad[0, :16, span].astype(f32) + stale * mom[0, :16, span]
-            + fresh * held[unit][:, :CHUNK].astype(f32))
-        new_ref[0, 16:, span] = (
-            grad[0, 16:, span].astype(f32) + stale * mom[0, 16:, span]
-            + fresh * unpack_rest(held[unit][:, CHUNK:].astype(f32)))
+def end_kernel(
+    lost_ref, back, live, grad, mom, new_ref, update_ref, bv, lv, gv, mv, uv, in_sem, out_sem,
+):
+    found = lost_ref[0] == 0
+
+    def in_copies(m):
+        t, j = m // 3, lax.rem(m, 3)
+        return [
+            pltpu.make_async_copy(grad.at[m], gv.at[m], in_sem.at[0, m]),
+            pltpu.make_async_copy(back.at[t, j], bv.at[t, j], in_sem.at[1, m]),
+            pltpu.make_async_copy(back.at[t, 3, :, j], bv.at[t, 3, :, j], in_sem.at[2, m]),
+        ]
+
+    def mom_copy(m):
+        return pltpu.make_async_copy(mom.at[m], mv.at[m], in_sem.at[3, m])
+
+    def live_copy():
+        return pltpu.make_async_copy(live, lv, in_sem.at[4, 0])
+
+    def out_copies(m):
+        return [
+            pltpu.make_async_copy(mv.at[m], new_ref.at[m], out_sem.at[0, m]),
+            pltpu.make_async_copy(uv.at[m], update_ref.at[m], out_sem.at[1, m]),
+        ]
+
+    @pl.when(jnp.logical_not(found))
+    def _():
+        live_copy().start()
+
+    def load(m, carry):
+        @pl.when(found)
+        def _():
+            mom_copy(m).start()
+
+        for copy in in_copies(m):
+            copy.start()
+        return carry
+
+    lax.fori_loop(0, MATS_GRP, load, 0)
+
+    @pl.when(jnp.logical_not(found))
+    def _():
+        live_copy().wait()
+
+    def unit(held, m, k):
+        t, j = m // 3, lax.rem(m, 3)
+        return held[t, j, k // 3, k % 3] if k < 6 else held[t, 3, k - 6, j]
+
+    def matrix(m, carry):
+        for copy in in_copies(m):
+            copy.wait()
+
+        @pl.when(found)
+        def _():
+            mom_copy(m).wait()
+            mv[m] = gv[m].astype(f32) + beta * mv[m]
+
+        @pl.when(jnp.logical_not(found))
+        def _():
+            for k in range(CHUNKS):
+                span = pl.ds(CHUNK * k, CHUNK)
+                held = unit(lv, m, k).astype(f32)
+                mv[m, :16, span] = gv[m, :16, span].astype(f32) + beta * held[:, :CHUNK]
+                mv[m, 16:, span] = (
+                    gv[m, 16:, span].astype(f32) + beta * unpack_rest(held[:, CHUNK:]))
+
+        for k in range(CHUNKS):
+            span = pl.ds(CHUNK * k, CHUNK)
+            returned = unit(bv, m, k)
+            uv[m, :16, span] = returned[:, :CHUNK]
+            uv[m, 16:, span] = unpack_rest(returned[:, CHUNK:].astype(f32)).astype(bf16)
+        for copy in out_copies(m):
+            copy.start()
+        return carry
+
+    lax.fori_loop(0, MATS_GRP, matrix, 0)
+
+    def drain(m, carry):
+        for copy in out_copies(m):
+            copy.wait()
+        return carry
+
+    lax.fori_loop(0, MATS_GRP, drain, 0)
 
 
 def local(grad, momentum, backup, recovery):
@@ -486,41 +567,26 @@
             pltpu.VMEM((R, R), bf16), pltpu.VMEM((R, R), bf16),
             pltpu.VMEM((R, R), bf16), pltpu.VMEM((R, R), bf16),
             dma((3, 16)), steps, steps, steps, steps, steps, steps, dma, dma, steps,
-            dma, dma, dma((3,)), dma((3,)), dma((3,)), dma, dma, dma,
+            dma((2,)), dma((2,)), dma((3,)), dma((3,)), dma((3,)), dma, dma, dma,
             dma((3, 5)), dma((3, 5)), dma((5,)), dma((3, 5)), dma, dma,
         ],
         compiler_params=pltpu.CompilerParams(
             collective_id=0, has_side_effects=True, vmem_limit_bytes=60 << 20),
     )(recovery, grad, momentum, backup)
 
-    def owner_block(m, scale=1):
-        return (m // 3 * scale, lax.rem(m, 3) * scale, 0, 0, 0, 0)
-
-    def hub_block(m, scale=1):
-        return (m // 3 * scale, 3, 0, lax.rem(m, 3) * scale, 0, 0)
-
-    owner_shape, hub_shape = (1, 1, 2, 3, 16, UNIT), (1, 1, 2, 1, 16, UNIT)
-    plain = pl.BlockSpec((1, ROWS_DEV, MODEL_WIDTH), lambda m, lost: (m, 0, 0))
     parted = (4, 4, 2, 3, 16, UNIT)
     return pl.pallas_call(
         end_kernel,
-        grid_spec=pltpu.PrefetchScalarGridSpec(
-            num_scalar_prefetch=1,
-            grid=(MATS_GRP,),
-            in_specs=[
-                pl.BlockSpec(owner_shape, lambda m, lost: owner_block(m)),
-                pl.BlockSpec(hub_shape, lambda m, lost: hub_block(m)),
-                pl.BlockSpec(owner_shape, lambda m, lost: owner_block(m, lost[0])),
-                pl.BlockSpec(hub_shape, lambda m, lost: hub_block(m, lost[0])),
-                plain,
-                pl.BlockSpec((1, ROWS_DEV, MODEL_WIDTH), lambda m, lost: (m * (1 - lost[0]), 0, 0)),
-            ],
-            out_specs=[plain, plain],
-        ),
         out_shape=[jax.ShapeDtypeStruct(shard, f32), jax.ShapeDtypeStruct(shard, bf16)],
+        in_specs=[scalars] + [anywhere] * 4,
+        out_specs=[anywhere] * 2,
+        scratch_shapes=[
+            pltpu.VMEM(parted, bf16), pltpu.VMEM(parted, bf16), pltpu.VMEM(shard, bf16),
+            pltpu.VMEM(shard, f32), pltpu.VMEM(shard, bf16),
+            dma((5, MATS_GRP)), dma((2, MATS_GRP)),
+        ],
         compiler_params=pltpu.CompilerParams(vmem_limit_bytes=60 << 20),
-    )(lost, returned.reshape(parted), returned.reshape(parted), live.reshape(parted),
-      live.reshape(parted), grad, momentum)
+    )(lost, returned.reshape(parted), live.reshape(parted), grad, momentum)
 
 
 def solution(mesh):

time: 150 us -> 144 us (0.960); the launches traced: 149 us -> 142 us
  Pallas kernels: 149 us -> 141 us
    pallas_call x1, Pallas kernels: 134 us -> 129 us  [local(): pl.pallas_call(main_kernel, out_shape=[jax.ShapeDtypeStruct(whole, bf16)]...]
    pallas_call x1, Pallas kernels: 14.8 us -> 11.3 us  [local(): pl.pallas_call(end_kernel, out_shape=[jax.ShapeDtypeStruct(shard, f32), j...]
where the time goes in v3:
time: 144 us; the launch traced here: 142 us
  Pallas kernels  141 us (98%)
    pallas_call x1, Pallas kernels, local(): pl.pallas_call(main_kernel, out_shape=[jax.ShapeDtypeStruct(whole, bf16)]...  129 us
    pallas_call x1, Pallas kernels, local(): pl.pallas_call(end_kernel, out_shape=[jax.ShapeDtypeStruct(shard, f32), j...  11.3 us

profile of v3, /device:TPU:33, one launch (start us, length us, event | category | flops | bytes accessed | tf_op | source)
XLA Modules:
  0.0 141.5 jit_solution(10926800916114249267)
XLA Ops:
  0.6 129.4 %shard_map.59 = (bf16[16,2,3,16,1024]{4,3,2,1,0:T(8,128)(2,1)}, bf16[16,2,3,16,1024]{4,3,2,1,0:T(8,128)(2,1)}, s32[1]{0:T(128)}) custom-call(s32[4]{0:T(128)} %recovery.1, bf16[12,18,7168]{2,1,0:T(8,128)(2,1)} %grad.3, f32[12,18,7168]{2,1,0:T(8,128)} %mom.3, f32[12,18,7168]{2,1,0:T(8,128)} %back.1), custom_call_target="tpu_custom_call" | custom-call | tf_op jit(solution)/shard_map/pallas_call | solution.py:554
  130.0 11.3 %shard_map.60 = (f32[12,18,7168]{2,1,0:T(8,128)}, bf16[12,18,7168]{2,1,0:T(8,128)(2,1)}) custom-call(s32[1]{0:T(128)} %get-tuple-element.5.lost_ref, bf16[4,4,2,3,16,1024]{5,4,3,2,1,0:T(8,128)(2,1)} %bitcast.2, bf16[4,4,2,3,16,1024]{5,4,3,2,1,0:T(8,128)(2,1)} %bitcast.3, bf16[12,18,7168]{2,1,0:T(8,128)(2,1)} %grad.3, f32[12,18,7168]{2,1,0:T(8,128)} %mom.3), custom_call_target="tpu_custom_call" | custom-call | tf_op jit(solution)/shard_map/pallas_call | solution.py:578

commit v4 on v3

--- a/solution.py
+++ b/solution.py
@@ -35,7 +35,7 @@
 FAR_FIRST = STEPS[:0:-1] + STEPS[:1]
 EVEN_STEPS = tuple(v for v in STEPS if sum(v) % 2 == 0)
 ODD_STEPS = tuple(v for v in STEPS if sum(v) % 2 == 1)
-HUBS_BEFORE = 8
+HUBS_BEFORE = 6
 
 
 def order_of(chip):

time: 144 us -> 144 us (level)
  no operation moved by 1% of the time
where the time goes in v4:
time: 144 us; the launch traced here: 143 us
  Pallas kernels  142 us (99%)
    pallas_call x1, Pallas kernels, local(): pl.pallas_call(main_kernel, out_shape=[jax.ShapeDtypeStruct(whole, bf16)]...  131 us
    pallas_call x1, Pallas kernels, local(): pl.pallas_call(end_kernel, out_shape=[jax.ShapeDtypeStruct(shard, f32), j...  11.3 us

profile of v4, /device:TPU:33, one launch (start us, length us, event | category | flops | bytes accessed | tf_op | source)
XLA Modules:
  0.0 142.7 jit_solution(9766890708619469237)
XLA Ops:
  0.6 130.5 %shard_map.59 = (bf16[16,2,3,16,1024]{4,3,2,1,0:T(8,128)(2,1)}, bf16[16,2,3,16,1024]{4,3,2,1,0:T(8,128)(2,1)}, s32[1]{0:T(128)}) custom-call(s32[4]{0:T(128)} %recovery.1, bf16[12,18,7168]{2,1,0:T(8,128)(2,1)} %grad.3, f32[12,18,7168]{2,1,0:T(8,128)} %mom.3, f32[12,18,7168]{2,1,0:T(8,128)} %back.1), custom_call_target="tpu_custom_call" | custom-call | tf_op jit(solution)/shard_map/pallas_call | solution.py:554
  131.2 11.3 %shard_map.60 = (f32[12,18,7168]{2,1,0:T(8,128)}, bf16[12,18,7168]{2,1,0:T(8,128)(2,1)}) custom-call(s32[1]{0:T(128)} %get-tuple-element.5.lost_ref, bf16[4,4,2,3,16,1024]{5,4,3,2,1,0:T(8,128)(2,1)} %bitcast.2, bf16[4,4,2,3,16,1024]{5,4,3,2,1,0:T(8,128)(2,1)} %bitcast.3, bf16[12,18,7168]{2,1,0:T(8,128)(2,1)} %grad.3, f32[12,18,7168]{2,1,0:T(8,128)} %mom.3), custom_call_target="tpu_custom_call" | custom-call | tf_op jit(solution)/shard_map/pallas_call | solution.py:578
